TPU v7x, 32 devices: a whole 2x2x4 slice. The times are simulated.
32 devices in a mesh: seq: 16 (over z, y, core), tp: 2 (over x).
Axes of the slice: x: 2, y: 2, z: 4, core: 2. Of those that a mesh axis runs over, the one named last changes fastest.
Arguments:
- q_proj: bfloat16 [2048, 8192], P('seq', 'tp'), may hold values from -6 to 6
- k_proj: bfloat16 [2048, 8192], P('seq', 'tp'), may hold values from -6 to 6
- v_proj: bfloat16 [2048, 8192], P('seq', 'tp'), may hold values from -6 to 6
- grad_out: bfloat16 [2048, 8192], P('seq', 'tp'), may hold values from -6 to 6
- w_first: float32 [32, 64], replicated, may hold values from -2 to 2
- w_second: float32 [64, 8192], P(None, 'tp'), may hold values from -0.75 to 0.75
- decay_rate: float32 [8192], P('tp'), may hold values from 0.02 to 64
- skip_gain: float32 [8192], P('tp'), may hold values from 0.5 to 1.5
Outputs:
- grad_q: bfloat16 [2048, 8192], P('seq', 'tp')
- grad_k: bfloat16 [2048, 8192], P('seq', 'tp')
- grad_v: bfloat16 [2048, 8192], P('seq', 'tp')
- grad_first: float32 [32, 64], replicated
- grad_second: float32 [64, 8192], P(None, 'tp')
- grad_decay: float32 [8192], P('tp')
- grad_skip: float32 [8192], P('tp')
All inputs are finite; a program needn't handle non-finite values.
Results may differ from a plain program's by a relative error of at most 0.0058.
Values may be sent and summed in bfloat16 or wider, within the bound.
No kernel may reach another device: no remote copies, remote signals or barrier semaphores. Data moves between devices by JAX's collectives and lax.ppermute only.
A program may use at most 128 MiB of HBM per device.

v0:
```python
import functools
import math

import jax
import jax.numpy as jnp
import ml_dtypes
import numpy as np
from jax import lax
from jax.experimental import pallas as pl
from jax.experimental.pallas import tpu as pltpu
from jax.sharding import PartitionSpec as P

HIGH = lax.Precision.HIGHEST
MIB = 1024 * 1024


def positional_table(length, band_count):
    positions = jnp.arange(length, dtype=jnp.int32)
    band_index = jnp.arange(band_count, dtype=jnp.int32)
    frequency = 3 * (band_index + 1) * (band_index + 1) + band_index
    phase_index = positions[:, None] * frequency[None, :] % length
    angles = phase_index.astype(jnp.float32) * (2.0 * math.pi / length)
    return jnp.concatenate([jnp.sin(angles), jnp.cos(angles)], axis=1)


@functools.lru_cache(maxsize=None)
def transform_tables(length, height):
    j = np.arange(height)
    angles = (j[:, None] * j[None, :] % height) * (2.0 * np.pi / height)
    cosine, sine = np.cos(angles), np.sin(angles)
    forward = np.concatenate(
        [np.concatenate([cosine, sine], axis=1), np.concatenate([-sine, cosine], axis=1)], axis=0
    )
    return np.stack([forward, forward.T / length]).astype(np.float32)


@functools.lru_cache(maxsize=None)
def twiddle_table(length, height, lane):
    parts = length // height
    r = np.arange(parts)[:, None]
    j = np.arange(height)[None, :]
    angles = (j * (4 * r + 1) % (4 * length)) * (2.0 * np.pi / (4 * length))
    both = np.concatenate([np.cos(angles), -np.sin(angles)], axis=1).astype(np.float32)
    return np.repeat(both[:, :, None], lane, axis=2)


def turn(value, cosine, sine):
    real, imag = value
    return (real * cosine - imag * sine, real * sine + imag * cosine)


def small_fft(values, sign):
    count = len(values)
    if count == 1:
        return values
    even = small_fft(values[0::2], sign)
    odd = small_fft(values[1::2], sign)
    first, second = [], []
    for k in range(count // 2):
        real, imag = odd[k]
        if k == 0:
            pass
        elif 4 * k == count:
            real, imag = (-imag, real) if sign > 0 else (imag, -real)
        elif 8 * k == count:
            half = math.sqrt(0.5)
            if sign > 0:
                real, imag = (real - imag) * half, (real + imag) * half
            else:
                real, imag = (real + imag) * half, (imag - real) * half
        elif 8 * k == 3 * count:
            half = math.sqrt(0.5)
            if sign > 0:
                real, imag = (real + imag) * -half, (real - imag) * half
            else:
                real, imag = (imag - real) * half, (real + imag) * -half
        else:
            angle = sign * 2.0 * math.pi * k / count
            real, imag = turn((real, imag), math.cos(angle), math.sin(angle))
        base_real, base_imag = even[k]
        first.append((base_real + real, base_imag + imag))
        second.append((base_real - real, base_imag - imag))
    return first + second


def parts_forward(values):
    count = len(values)
    turned = []
    for p, value in enumerate(values):
        angle = 2.0 * math.pi * p / (4 * count)
        turned.append((value * math.cos(angle), value * -math.sin(angle)))
    return small_fft(turned, -1)


def parts_inverse(values):
    count = len(values)
    result = []
    for p, (real, imag) in enumerate(small_fft(values, 1)):
        angle = 2.0 * math.pi * p / (4 * count)
        result.append(real * math.cos(angle) - imag * math.sin(angle))
    return result


def split_table(table_ref, split_ref):
    table = table_ref[...]
    high = table.astype(jnp.bfloat16)
    split_ref[0] = high
    split_ref[1] = (table - high.astype(jnp.float32)).astype(jnp.bfloat16)


def dot_three(split_ref, direction, value):
    high, low = split_ref[0, direction], split_ref[1, direction]
    value_high = value.astype(jnp.bfloat16)
    value_low = (value - value_high.astype(jnp.float32)).astype(jnp.bfloat16)
    dot = functools.partial(jnp.dot, preferred_element_type=jnp.float32)
    return dot(high, value_high) + (dot(high, value_low) + dot(low, value_high))


def spectrum_product(left, right, height, conjugate):
    left_real, left_imag = left[:height], left[height:]
    right_real, right_imag = right[:height], right[height:]
    if conjugate:
        return jnp.concatenate(
            [
                left_real * right_real + left_imag * right_imag,
                left_real * right_imag - left_imag * right_real,
            ],
            axis=0,
        )
    return jnp.concatenate(
        [
            left_real * right_real - left_imag * right_imag,
            left_real * right_imag + left_imag * right_real,
        ],
        axis=0,
    )


def lane_slices(width):
    lane = min(width, 128)
    return [slice(at, at + lane) for at in range(0, width, lane)]


def first_chunk(load, work, twiddle_ref, index):
    parts, height = work.shape[0], work.shape[1] // 2
    row = pl.multiple_of(index * 16, 16)
    for lanes in lane_slices(work.shape[2]):
        values = [load(p, row, lanes) for p in range(parts)]
        for half in (0, 8):
            upper = pl.ds(row + half, 8)
            lower = pl.ds(height + row + half, 8)
            turned = parts_forward([value[half : half + 8] for value in values])
            for r, value in enumerate(turned):
                real, imag = turn(value, twiddle_ref[r, upper, :], twiddle_ref[r, lower, :])
                work[r, upper, lanes] = real
                work[r, lower, lanes] = imag


def last_chunk(store, work, twiddle_ref, index):
    parts, height = work.shape[0], work.shape[1] // 2
    row = pl.multiple_of(index * 16, 16)
    for lanes in lane_slices(work.shape[2]):
        halves = []
        for half in (0, 8):
            upper = pl.ds(row + half, 8)
            lower = pl.ds(height + row + half, 8)
            values = [
                turn(
                    (work[r, upper, lanes], work[r, lower, lanes]),
                    twiddle_ref[r, upper, :],
                    -twiddle_ref[r, lower, :],
                )
                for r in range(parts)
            ]
            halves.append(parts_inverse(values))
        for p in range(parts):
            store(p, row, lanes, jnp.concatenate([halves[0][p], halves[1][p]], axis=0))


def run_chunks(height, chunk, parts=0, block=None):
    chunks = height // 16
    group = parts // chunks if parts % chunks == 0 else 0

    def one(index, carry):
        for b in range(group):
            block(index * group + b)
        chunk(index)
        return carry

    lax.fori_loop(0, chunks, one, 0)
    if group == 0 and parts > 0:
        run_blocks(parts, block)


def run_blocks(parts, block):
    def one(index, carry):
        block(index)
        return carry

    lax.fori_loop(0, parts, one, 0)


def envelope_at(decay, row, length, shape):
    position = (row + lax.broadcasted_iota(jnp.int32, shape, 0)).astype(jnp.float32)
    fraction = position * (1.0 / length)
    return jnp.exp(-decay * fraction), fraction


def filter_kernel(
    hidden_ref, w_ref, decay_ref, table_ref, twiddle_ref, filter_ref, spectrum_ref, work, split
):
    parts, height = work.shape[0], work.shape[1] // 2
    length = filter_ref.shape[0]
    scale = length**-0.5
    split_table(table_ref, split)
    filter_ref[...] = jnp.dot(
        hidden_ref[...], w_ref[...], precision=HIGH, preferred_element_type=jnp.float32
    )

    def load(p, row, lanes):
        rows = pl.ds(pl.multiple_of(p * height + row, 16), 16)
        raw = filter_ref[rows, lanes]
        envelope, _ = envelope_at(decay_ref[:, lanes], p * height + row, length, raw.shape)
        value = raw * envelope * scale
        filter_ref[rows, lanes] = value
        return value

    def block(r):
        spectrum_ref[r] = dot_three(split, 0, work[r])

    run_chunks(height, lambda i: first_chunk(load, work, twiddle_ref, i))
    run_blocks(parts, block)


def main_kernel(
    both_ref,
    h_any,
    table_ref,
    twiddle_ref,
    skip_ref,
    back_ref,
    cross_any,
    work_in,
    work_grad,
    cross,
    h,
    split,
    sems,
):
    parts, height = work_in.shape[0], work_in.shape[1] // 2
    copy_in = pltpu.make_async_copy(h_any, h, sems.at[0])
    copy_in.start()
    split_table(table_ref, split)

    def load_from(which):
        def load(p, row, lanes):
            return both_ref[p, which, pl.ds(row, 16), lanes].astype(jnp.float32)

        return load

    def store_to(which):
        load = load_from(which)

        def store(p, row, lanes, value):
            value = value + skip_ref[:, lanes] * load(p, row, lanes)
            back_ref[p, which, pl.ds(row, 16), lanes] = value.astype(jnp.bfloat16)

        return store

    def block_in(r):
        spectrum = dot_three(split, 0, work_in[r])
        cross[r] = spectrum
        work_in[r] = dot_three(split, 1, spectrum_product(h[r], spectrum, height, False))

    def block_grad(r):
        spectrum = dot_three(split, 0, work_grad[r])
        cross[r] = spectrum_product(cross[r], spectrum, height, True)
        work_grad[r] = dot_three(split, 1, spectrum_product(h[r], spectrum, height, True))

    run_chunks(height, lambda i: first_chunk(load_from(0), work_in, twiddle_ref, i))
    copy_in.wait()
    run_chunks(
        height, lambda i: first_chunk(load_from(1), work_grad, twiddle_ref, i), parts, block_in
    )
    run_chunks(
        height, lambda i: last_chunk(store_to(0), work_in, twiddle_ref, i), parts, block_grad
    )
    copy_out = pltpu.make_async_copy(cross, cross_any, sems.at[1])
    copy_out.start()
    run_chunks(height, lambda i: last_chunk(store_to(1), work_grad, twiddle_ref, i))
    copy_out.wait()


def filter_grad_kernel(
    both_ref,
    cross_ref,
    table_ref,
    twiddle_ref,
    decay_ref,
    filter_ref,
    hidden_t_ref,
    w_t_ref,
    cosine_ref,
    positional_t_ref,
    small_ref,
    first_ref,
    work,
    raw,
    sums,
    split,
):
    parts, height = work.shape[0], work.shape[1] // 2
    length, width = raw.shape
    hidden_count = hidden_t_ref.shape[0]
    band_total = positional_t_ref.shape[0]
    scale = length**-0.5
    split_table(table_ref, split)
    sums[...] = jnp.zeros_like(sums)

    def block(r):
        work[r] = dot_three(split, 1, cross_ref[r])

    def store(p, row, lanes, value):
        rows = pl.ds(pl.multiple_of(p * height + row, 16), 16)
        envelope, fraction = envelope_at(
            decay_ref[:, lanes], p * height + row, length, value.shape
        )
        both = value * filter_ref[rows, lanes] * fraction
        sums[1, :, lanes] += both[:8] + both[8:]
        raw[rows, lanes] = value * envelope * scale
        left = both_ref[p, 0, pl.ds(row, 16), lanes].astype(jnp.float32)
        right = both_ref[p, 1, pl.ds(row, 16), lanes].astype(jnp.float32)
        both = left * right
        sums[0, :, lanes] += both[:8] + both[8:]

    run_blocks(parts, block)
    run_chunks(height, lambda i: last_chunk(store, work, twiddle_ref, i))

    dot = functools.partial(jnp.dot, precision=HIGH, preferred_element_type=jnp.float32)
    second = jnp.zeros((hidden_count, width), jnp.float32)
    first = jnp.zeros((band_total, hidden_count), jnp.float32)
    chunk = min(length, 512)
    for at in range(0, length, chunk):
        rows = slice(at, at + chunk)
        grad_raw = raw[rows, :]
        second += dot(hidden_t_ref[:, rows], grad_raw)
        hidden_part = dot(grad_raw, w_t_ref[...])
        first += dot(positional_t_ref[:, rows], hidden_part * cosine_ref[rows, :])

    def high_low(value):
        high = value.astype(jnp.bfloat16)
        low = (value - high.astype(jnp.float32)).astype(jnp.bfloat16)
        return high.astype(jnp.float32), low.astype(jnp.float32)

    high, low = high_low(first * scale)
    first_ref[:band_total, :] = high.astype(jnp.bfloat16)
    first_ref[band_total:, :] = low.astype(jnp.bfloat16)
    small_ref[:hidden_count, :] = (second * scale).astype(jnp.bfloat16)
    place = lax.broadcasted_iota(jnp.int32, (16, width), 0)
    tail = jnp.zeros((16, width), jnp.float32)
    decay_pair = high_low(jnp.sum(sums[1], axis=0, keepdims=True) * -scale)
    skip_pair = high_low(jnp.sum(sums[0], axis=0, keepdims=True) * scale)
    for at, row in enumerate(decay_pair + skip_pair):
        tail = jnp.where(place == at, row, tail)
    small_ref[hidden_count:, :] = tail.astype(jnp.bfloat16)


def params(limit):
    return pltpu.CompilerParams(vmem_limit_bytes=limit)


def estimate(flops, nbytes):
    return pl.CostEstimate(flops=flops, bytes_accessed=nbytes, transcendentals=0)


def gate_kernel(*refs):
    out_ref = refs[-1]
    width = out_ref.shape[3]
    for at in range(out_ref.shape[0]):
        lanes = slice(at * width, (at + 1) * width)
        for which in range(2):
            left = refs[2 * which][:, lanes].astype(jnp.float32)
            right = refs[2 * which + 1][:, lanes].astype(jnp.float32)
            out_ref[at, which] = (left * right).astype(jnp.bfloat16)


def gate(factors, count):
    rows, columns = factors[0].shape
    width = columns // count
    if width % 128 != 0:
        pairs = []
        for left, right in (factors[:2], factors[2:]):
            product = (left.astype(jnp.float32) * right.astype(jnp.float32)).astype(jnp.bfloat16)
            pairs.append(product.reshape(rows, count, width).transpose(1, 0, 2))
        return jnp.stack(pairs, axis=1)
    group = math.gcd(count, 4)
    return pl.pallas_call(
        gate_kernel,
        grid=(count // group,),
        in_specs=[pl.BlockSpec((rows, group * width), lambda i: (0, i))] * 4,
        out_specs=pl.BlockSpec((group, 2, rows, width), lambda i: (i, 0, 0, 0)),
        out_shape=jax.ShapeDtypeStruct((count, 2, rows, width), jnp.bfloat16),
        compiler_params=params(16 * MIB),
        cost_estimate=estimate(2 * rows * columns, rows * columns * 12),
    )(*factors)


def ungate_kernel(back_ref, g_ref, v_ref, k_ref, q_out, k_out, v_out):
    width = back_ref.shape[3]
    for at in range(back_ref.shape[0]):
        lanes = slice(at * width, (at + 1) * width)
        for which, factor_ref, out_ref in (
            (0, g_ref, q_out),
            (1, v_ref, k_out),
            (1, k_ref, v_out),
        ):
            back = back_ref[at, which].astype(jnp.float32)
            factor = factor_ref[:, lanes].astype(jnp.float32)
            out_ref[:, lanes] = (back * factor).astype(jnp.bfloat16)


def ungate(back, factors):
    count, _, rows, width = back.shape
    columns = count * width
    if width % 128 != 0:
        outs = []
        for which, factor in zip((0, 1, 1), factors):
            part = back[:, which].transpose(1, 0, 2).reshape(rows, columns).astype(jnp.float32)
            outs.append((part * factor.astype(jnp.float32)).astype(jnp.bfloat16))
        return outs
    group = math.gcd(count, 4)
    wide = pl.BlockSpec((rows, group * width), lambda i: (0, i))
    return pl.pallas_call(
        ungate_kernel,
        grid=(count // group,),
        in_specs=[pl.BlockSpec((group, 2, rows, width), lambda i: (i, 0, 0, 0))] + [wide] * 3,
        out_specs=[wide] * 3,
        out_shape=[jax.ShapeDtypeStruct((rows, columns), jnp.bfloat16)] * 3,
        compiler_params=params(16 * MIB),
        cost_estimate=estimate(3 * rows * columns, rows * columns * 16),
    )(back, *factors)


def per_device(q_proj, k_proj, v_proj, grad_out, w_first, w_second, decay_rate, skip_gain):
    height, chan_tp = q_proj.shape
    parts = lax.axis_size("seq")
    length = height * parts
    width = chan_tp // parts
    band_total, hidden_count = w_first.shape
    seq_index = lax.axis_index("seq")

    def exchange(values):
        return lax.all_to_all(values, "seq", split_axis=0, concat_axis=0, tiled=True)

    both = exchange(gate((k_proj, v_proj, grad_out, q_proj), parts))

    tables = jnp.asarray(transform_tables(length, height))
    twiddle = jnp.asarray(twiddle_table(length, height, min(width, 128)))
    positional = positional_table(length, band_total // 2)
    sine_input = jnp.dot(positional, w_first, precision=HIGH, preferred_element_type=jnp.float32)
    hidden = jnp.sin(sine_input)
    cosine = jnp.cos(sine_input)
    offset = seq_index * width
    w_mine = lax.dynamic_slice_in_dim(w_second, offset, width, 1)
    decay_mine = lax.dynamic_slice_in_dim(decay_rate, offset, width, 0)[None, :]
    skip_mine = lax.dynamic_slice_in_dim(skip_gain, offset, width, 0)[None, :]

    spectrum_shape = jax.ShapeDtypeStruct((parts, 2 * height, width), jnp.float32)
    work = pltpu.VMEM(spectrum_shape.shape, jnp.float32)
    split = pltpu.VMEM((2,) + tables.shape, jnp.bfloat16)
    anywhere = pl.BlockSpec(memory_space=pl.ANY)
    in_vmem = pl.BlockSpec(memory_space=pltpu.VMEM)
    product_flops = 2 * 3 * parts * 4 * height * height * width
    limit = 32 * MIB if length * max(width, 128) <= 2048 * 256 else 58 * MIB

    long_filter, filter_spectrum = pl.pallas_call(
        filter_kernel,
        in_specs=[in_vmem] * 5,
        out_specs=[in_vmem, in_vmem],
        out_shape=[jax.ShapeDtypeStruct((length, width), jnp.float32), spectrum_shape],
        scratch_shapes=[work, split],
        compiler_params=params(limit),
        cost_estimate=estimate(product_flops, length * width * 12),
    )(hidden, w_mine, decay_mine, tables, twiddle)

    back, cross = pl.pallas_call(
        main_kernel,
        in_specs=[in_vmem, anywhere, in_vmem, in_vmem, in_vmem],
        out_specs=[in_vmem, anywhere],
        out_shape=[jax.ShapeDtypeStruct(both.shape, jnp.bfloat16), spectrum_shape],
        scratch_shapes=[work, work, work, work, split, pltpu.SemaphoreType.DMA((2,))],
        compiler_params=params(limit),
        cost_estimate=estimate(4 * product_flops, length * width * 32),
    )(both, filter_spectrum, tables, twiddle, skip_mine)
    back = exchange(back)

    small, first_pair = pl.pallas_call(
        filter_grad_kernel,
        in_specs=[in_vmem] * 10,
        out_specs=[in_vmem, in_vmem],
        out_shape=[
            jax.ShapeDtypeStruct((hidden_count + 16, width), jnp.bfloat16),
            jax.ShapeDtypeStruct((2 * band_total, hidden_count), jnp.bfloat16),
        ],
        scratch_shapes=[
            work,
            pltpu.VMEM((length, width), jnp.float32),
            pltpu.VMEM((2, 8, width), jnp.float32),
            split,
        ],
        compiler_params=params(limit),
        cost_estimate=estimate(2 * product_flops, length * width * 30),
    )(
        both,
        cross,
        tables,
        twiddle,
        decay_mine,
        long_filter,
        hidden.T,
        w_mine.T,
        cosine,
        positional.T,
    )
    packed = jnp.concatenate([small, first_pair.reshape(-1, width)], axis=0)
    gathered = lax.all_gather(packed, "seq", axis=1, tiled=True).astype(jnp.float32)
    grad_second = gathered[:hidden_count]
    grad_decay = gathered[hidden_count] + gathered[hidden_count + 1]
    grad_skip = gathered[hidden_count + 2] + gathered[hidden_count + 3]
    first_rows = gathered[hidden_count + 16 :].reshape(-1, parts, width).sum(axis=1)
    grad_first = first_rows.reshape(2, band_total, hidden_count).sum(axis=0)
    if lax.axis_size("tp") == 2:
        grad_first = grad_first + lax.ppermute(grad_first, "tp", [(0, 1), (1, 0)])
    else:
        grad_first = lax.psum(grad_first, "tp")
    grad_q, grad_k, grad_v = ungate(back, (grad_out, v_proj, k_proj))
    return (grad_q, grad_k, grad_v, grad_first, grad_second, grad_decay, grad_skip)


def solution(mesh):
    return jax.shard_map(
        per_device,
        mesh=mesh,
        in_specs=(
            P("seq", "tp"),
            P("seq", "tp"),
            P("seq", "tp"),
            P("seq", "tp"),
            P(),
            P(None, "tp"),
            P("tp"),
            P("tp"),
        ),
        out_specs=(
            P("seq", "tp"),
            P("seq", "tp"),
            P("seq", "tp"),
            P(),
            P(None, "tp"),
            P("tp"),
            P("tp"),
        ),
        check_vma=False,
    )
```

profile of v0, /device:TPU:0, one launch (start us, length us, event | category | flops | bytes accessed | tf_op | source)
XLA Modules:
  0.0 170.0 jit_solution(7778411068580310424)
XLA Ops:
  0.7 1.3 copy-done.6
  2.0 1.2 copy-done.8
  3.2 1.2 copy-done.10
  4.4 1.2 copy-done.19
  6.5 1.4 copy-done.1
  7.9 7.5 %all-to-all-start = ((bf16[16,2,128,256]{3,2,1,0:T(8,128)(2,1)}), bf16[16,2,128,256]{3,2,1,0:T(8,128)(2,1)S(1)}, u32[]{:S(2)}, u32[]{:S(2)}) async-start(bf16[16,2,128,256]{3,2,1,0:T(8,128)(2,1)} %copy-done.1), calls=%async_computation | async-start | bytes 4194304 | tf_op jit(solution)/shard_map/all_to_all | solution.py:453
  16.1 3.5 %fusion.11 = (f32[2048,64]{0,1:T(8,128)}, f32[2048,64]{0,1:T(8,128)}) fusion(f32[32,64]{1,0:T(8,128)S(1)} %copy-done.27, f32[2048,16]{0,1:T(8,128)S(1)} %get-tuple-element.30, f32[2048,16]{0,1:T(8,128)S(1)} %get-tuple-element.29), kind=kOutput, calls=%fused_computation.23 | convolution fusion | flops 50397184 | bytes 1318912 | tf_op jit(solution)/shard_map/dot_general | solution.py:460
  19.5 2.4 %copy.26.hidden_ref = f32[2048,64]{1,0:T(8,128)} copy(f32[2048,64]{0,1:T(8,128)} %get-tuple-element.28) | data formatting | bytes 1048576 | tf_op jit(solution)/shard_map/sin | solution.py:461
  23.4 1.6 copy-done.12
  25.0 1.2 copy-done.18
  27.3 8.7 %shard_map.154 = (f32[2048,256]{1,0:T(8,128)S(1)}, f32[16,256,256]{2,1,0:T(8,128)S(1)}) custom-call(f32[2048,64]{1,0:T(8,128)S(1)} %copy-done.18, f32[64,256]{1,0:T(8,128)S(1)} %constant_dynamic-slice_fusion.w_ref, f32[1,256]{1,0:T(1,128)S(1)} %bitcast.14, f32[2,256,256]{2,1,0:T(8,128)S(1)} %copy-done.20, f32[16,256,128]{2,1,0:T(8,128)S(1)} %copy-done.12), custom_call_target="tpu_custom_call" | custom-call | flops 1610612736 | bytes 6291456 | tf_op jit(solution)/shard_map/pallas_call | solution.py:476
  36.0 1.4 copy-done.15
  37.4 2.0 %copy-done.23 = f32[16,256,256]{2,1,0:T(8,128)} copy-done((f32[16,256,256]{2,1,0:T(8,128)}, f32[16,256,256]{2,1,0:T(8,128)S(1)}, u32[]{:S(2)}) %copy-start.23) | copy-done | bytes 4194328
  39.4 17.2 %all-to-all-done.both_ref = bf16[16,2,128,256]{3,2,1,0:T(8,128)(2,1)S(1)} async-done(((bf16[16,2,128,256]{3,2,1,0:T(8,128)(2,1)}), bf16[16,2,128,256]{3,2,1,0:T(8,128)(2,1)S(1)}, u32[]{:S(2)}, u32[]{:S(2)}) %all-to-all-start) | async-done | bytes 2097184 | tf_op jit(solution)/shard_map/all_to_all | solution.py:453
  56.5 1.6 copy-done.13
  59.2 2.2 %copy-done.24 = f32[16,256,256]{2,1,0:T(8,128)S(1)} copy-done((f32[16,256,256]{2,1,0:T(8,128)S(1)}, f32[16,256,256]{2,1,0:T(8,128)}, u32[]{:S(2)}) %copy-start.24) | copy-done | bytes 4194328
  61.4 22.6 %shard_map.155 = (bf16[16,2,128,256]{3,2,1,0:T(8,128)(2,1)S(1)}, f32[16,256,256]{2,1,0:T(8,128)S(1)}) custom-call(bf16[16,2,128,256]{3,2,1,0:T(8,128)(2,1)S(1)} %all-to-all-done.both_ref, f32[16,256,256]{2,1,0:T(8,128)S(1)} %copy-done.24, f32[2,256,256]{2,1,0:T(8,128)S(1)} %copy-done.21, f32[16,256,128]{2,1,0:T(8,128)S(1)} %copy-done.13, f32[1,256]{1,0:T(1,128)S(1)} %bitcast.16), custom_call_target="tpu_custom_call" | custom-call | flops 6442450944 | bytes 16777216 | tf_op jit(solution)/shard_map/pallas_call | solution.py:486
  84.0 1.9 %copy-done.3 = f32[16,256,256]{2,1,0:T(8,128)} copy-done((f32[16,256,256]{2,1,0:T(8,128)}, f32[16,256,256]{2,1,0:T(8,128)S(1)}, u32[]{:S(2)}) %copy-start.3) | copy-done | bytes 4194328
  85.9 1.4 copy-done.17
  87.3 11.3 %all-to-all-start.1 = ((bf16[16,2,128,256]{3,2,1,0:T(8,128)(2,1)}), bf16[16,2,128,256]{3,2,1,0:T(8,128)(2,1)}, u32[]{:S(2)}, u32[]{:S(2)}) async-start(bf16[16,2,128,256]{3,2,1,0:T(8,128)(2,1)} %copy-done.17), calls=%async_computation.1 | async-start | bytes 4194304 | tf_op jit(solution)/shard_map/all_to_all | solution.py:453
  98.7 2.4 %copy.28.cosine_ref = f32[2048,64]{1,0:T(8,128)} copy(f32[2048,64]{0,1:T(8,128)} %get-tuple-element.27) | data formatting | bytes 1048576 | tf_op jit(solution)/shard_map/cos | solution.py:462
  103.0 2.2 %copy-done.4 = f32[16,256,256]{2,1,0:T(8,128)S(1)} copy-done((f32[16,256,256]{2,1,0:T(8,128)S(1)}, f32[16,256,256]{2,1,0:T(8,128)}, u32[]{:S(2)}) %copy-start.4) | copy-done | bytes 4194328
  105.2 1.2 copy-done.5
  106.4 1.6 copy-done.14
  108.0 1.6 copy-done.16
  110.7 11.4 %shard_map.157 = (bf16[80,256]{1,0:T(8,128)(2,1)S(1)}, bf16[64,64]{1,0:T(8,128)(2,1)S(1)}) custom-call(bf16[16,2,128,256]{3,2,1,0:T(8,128)(2,1)S(1)} %all-to-all-done.both_ref, f32[16,256,256]{2,1,0:T(8,128)S(1)} %copy-done.4, f32[2,256,256]{2,1,0:T(8,128)S(1)} %copy-done.22, f32[16,256,128]{2,1,0:T(8,128)S(1)} %copy-done.14, f32[1,256]{1,0:T(1,128)S(1)} %bitcast.15, ...), custom_call_target="tpu_custom_call" | custom-call | flops 3221225472 | bytes 15728640 | tf_op jit(solution)/shard_map/pallas_call | solution.py:497
  122.2 34.7 %all_gather.3 = bf16[96,4096]{1,0:T(8,128)(2,1)S(1)} all-gather(bf16[96,256]{1,0:T(8,128)(2,1)S(1)} %pad_maximum_fusion.2), channel_id=1, replica_groups=mesh['seq'=16,'tp'=2] {'seq'}, dimensions={1}, use_global_device_ids=true | all-gather | bytes 835584 | tf_op jit(solution)/shard_map/all_gather | solution.py:526
  156.9 1.4 convert_element_type.9
  158.6 1.6 collective-permute-start
  160.2 1.9 %slice_add_fusion = (f32[1,4096]{1,0:T(1,128)}, f32[1,4096]{1,0:T(1,128)}) fusion(f32[96,4096]{1,0:T(8,128)} %convert_element_type.9), kind=kLoop, calls=%fused_computation.16 | loop fusion | flops 8192 | bytes 98304 | tf_op jit(solution)/shard_map/add | solution.py:529
  162.0 2.1 %slice.25 = f32[64,4096]{1,0:T(8,128)} slice(bf16[96,4096]{1,0:T(8,128)(2,1)} %copy-done.25), slice={[0:64], [0:4096]} | slice | bytes 2097152 | tf_op jit(solution)/shard_map/slice | solution.py:527
  166.0 4.0 %shard_map.156 = (bf16[128,4096]{1,0:T(8,128)(2,1)}, bf16[128,4096]{1,0:T(8,128)(2,1)}, bf16[128,4096]{1,0:T(8,128)(2,1)}) custom-call(bf16[16,2,128,256]{3,2,1,0:T(8,128)(2,1)} %all-to-all-done.1.back_ref, bf16[128,4096]{1,0:T(8,128)(2,1)S(1)} %copy-done.11, bf16[128,4096]{1,0:T(8,128)(2,1)S(1)} %copy-done.9, bf16[128,4096]{1,0:T(8,128)(2,1)S(1)} %copy-done.7), custom_call_target="tpu_custom_call" | custom-call | flops 1572864 | bytes 8388608 | tf_op jit(solution)/shard_map/pallas_call | solution.py:433
  (57 shorter events, 10.4 us)
Async XLA Ops:
  0.6 22.8 %copy-start = (f32[64,4096]{1,0:T(8,128)S(1)}, f32[64,4096]{1,0:T(8,128)}, u32[]{:S(2)}) copy-start(f32[64,4096]{1,0:T(8,128)} %param.15) | copy-start | bytes 3145732
  0.6 1.3 copy-start.6
  2.0 1.2 copy-start.8
  3.2 1.2 copy-start.10
  4.4 1.2 copy-start.19
  6.5 1.4 copy-start.1
  7.9 8.2 %copy-start.27 = (f32[32,64]{1,0:T(8,128)S(1)}, f32[32,64]{1,0:T(8,128)}, u32[]{:S(2)}) copy-start(f32[32,64]{1,0:T(8,128)} %param.14) | copy-start | bytes 24580
  7.9 48.6 %all-to-all-start = ((bf16[16,2,128,256]{3,2,1,0:T(8,128)(2,1)}), bf16[16,2,128,256]{3,2,1,0:T(8,128)(2,1)S(1)}, u32[]{:S(2)}, u32[]{:S(2)}) async-start(bf16[16,2,128,256]{3,2,1,0:T(8,128)(2,1)} %copy-done.1), calls=%async_computation | async-start | bytes 4194304 | tf_op jit(solution)/shard_map/all_to_all | solution.py:453
  16.1 5.8 %copy-start.26 = (f32[2048,16]{0,1:T(8,128)}, f32[2048,16]{0,1:T(8,128)S(1)}, u32[]{:S(2)}) copy-start(f32[2048,16]{0,1:T(8,128)S(1)} %get-tuple-element.30) | copy-start | bytes 393220
  23.4 1.6 copy-start.12
  25.0 1.2 copy-start.18
  26.2 1.0 copy-start.20
  36.0 1.4 copy-start.15
  37.4 2.0 %copy-start.23 = (f32[16,256,256]{2,1,0:T(8,128)}, f32[16,256,256]{2,1,0:T(8,128)S(1)}, u32[]{:S(2)}) copy-start(f32[16,256,256]{2,1,0:T(8,128)S(1)} %get-tuple-element.16.h_any) | copy-start | bytes 12582916
  56.5 1.6 copy-start.13
  58.1 1.0 copy-start.21
  59.2 2.2 %copy-start.24 = (f32[16,256,256]{2,1,0:T(8,128)S(1)}, f32[16,256,256]{2,1,0:T(8,128)}, u32[]{:S(2)}) copy-start(f32[16,256,256]{2,1,0:T(8,128)} %copy-done.23) | copy-start | bytes 12582916
  84.0 2.0 %copy-start.3 = (f32[16,256,256]{2,1,0:T(8,128)}, f32[16,256,256]{2,1,0:T(8,128)S(1)}, u32[]{:S(2)}) copy-start(f32[16,256,256]{2,1,0:T(8,128)S(1)} %get-tuple-element.21.cross_ref) | copy-start | bytes 12582916
  85.9 1.4 copy-start.17
  87.3 77.4 %all-to-all-start.1 = ((bf16[16,2,128,256]{3,2,1,0:T(8,128)(2,1)}), bf16[16,2,128,256]{3,2,1,0:T(8,128)(2,1)}, u32[]{:S(2)}, u32[]{:S(2)}) async-start(bf16[16,2,128,256]{3,2,1,0:T(8,128)(2,1)} %copy-done.17), calls=%async_computation.1 | async-start | bytes 4194304 | tf_op jit(solution)/shard_map/all_to_all | solution.py:453
  102.0 1.0 copy-start.2
  103.0 2.2 %copy-start.4 = (f32[16,256,256]{2,1,0:T(8,128)S(1)}, f32[16,256,256]{2,1,0:T(8,128)}, u32[]{:S(2)}) copy-start(f32[16,256,256]{2,1,0:T(8,128)} %copy-done.3) | copy-start | bytes 12582916
  105.2 1.2 copy-start.5
  106.4 1.6 copy-start.14
  108.0 1.6 copy-start.16
  109.6 1.0 copy-start.22
  156.9 1.4 copy-start.25
  158.4 6.4 %copy-start.7 = (bf16[128,4096]{1,0:T(8,128)(2,1)S(1)}, bf16[128,4096]{1,0:T(8,128)(2,1)}, u32[]{:S(2)}) copy-start(bf16[128,4096]{1,0:T(8,128)(2,1)} %k_ref.1) | copy-start | bytes 3145732
  158.4 6.4 %copy-start.9 = (bf16[128,4096]{1,0:T(8,128)(2,1)S(1)}, bf16[128,4096]{1,0:T(8,128)(2,1)}, u32[]{:S(2)}) copy-start(bf16[128,4096]{1,0:T(8,128)(2,1)} %v_ref.1) | copy-start | bytes 3145732
  158.6 5.5 %collective-permute-start = (f32[32,64]{1,0:T(8,128)S(1)}, f32[32,64]{1,0:T(8,128)S(1)}, u32[]{:S(2)}, u32[]{:S(2)}) collective-permute-start(f32[32,64]{1,0:T(8,128)S(1)} %reduce_sum.19), channel_id=1, source_target_pairs={{0,1},{1,0},{2,3},{3,2},{4,5},{5,4},{6,7},{7,6},{8,9},{9,8},{10,11... | collective-permute-start | bytes 24584 | tf_op jit(solution)/shard_map/ppermute | solution.py:533
  164.8 1.2 copy-start.11
where the time goes:
time: 172 us; the launch traced here: 170 us
  Pallas kernels  47.7 us (28%)
  local copies, waits for them, and re-layouts  40.3 us (23%)
  blocking collectives  34.7 us (20%)
  starting transfers between devices  20.3 us (12%)
  waiting for transfers between devices  17.2 us (10%)
  other arithmetic  5.49 us (3%)
  matrix products  3.45 us (2%)
    all_gather x1, blocking collectives, per_device(): lax.all_gather(packed, 'seq', axis=1, tiled=True).astype(jnp.float32)  34.7 us
    unnamed x58, local copies, waits for them, and re-layouts  31.8 us
    pallas_call x1, Pallas kernels, per_device(): pl.pallas_call(main_kernel, in_specs=[in_vmem, anywhere, in_vmem, in_vmem...  22.6 us
    all_to_all x2, starting transfers between devices, exchange(): lax.all_to_all(values, 'seq', split_axis=0, concat_axis=0, tiled=True)  18.8 us
    all_to_all x2, waiting for transfers between devices, exchange(): lax.all_to_all(values, 'seq', split_axis=0, concat_axis=0, tiled=True)  17.2 us
    pallas_call x1, Pallas kernels, per_device(): pl.pallas_call(filter_grad_kernel, in_specs=[in_vmem] * 10, out_specs=[in...  11.4 us
    pallas_call x1, Pallas kernels, per_device(): pl.pallas_call(filter_kernel, in_specs=[in_vmem] * 5, out_specs=[in_vmem,...  8.73 us
    pallas_call x1, Pallas kernels, ungate(): pl.pallas_call(ungate_kernel, grid=(count // group,), in_specs=[pl.BlockS...  4.03 us
  transfers between devices with their start and end apart: 3, of which 1 were waited for; matrix products, arithmetic and copies ran while one was open for 10% of the time, Pallas kernels for 12%

commit v1 on v0

v1 whole, which is shorter than its diff:
```python
import functools
import math

import jax
import jax.numpy as jnp
import ml_dtypes
import numpy as np
from jax import lax
from jax.experimental import pallas as pl
from jax.experimental.pallas import tpu as pltpu
from jax.sharding import PartitionSpec as P

HIGH = lax.Precision.HIGHEST
MIB = 1024 * 1024


def positional_table(length, band_count):
    positions = jnp.arange(length, dtype=jnp.int32)
    band_index = jnp.arange(band_count, dtype=jnp.int32)
    frequency = 3 * (band_index + 1) * (band_index + 1) + band_index
    phase_index = frequency[:, None] * positions[None, :] % length
    angles = phase_index.astype(jnp.float32) * (2.0 * math.pi / length)
    return jnp.concatenate([jnp.sin(angles), jnp.cos(angles)], axis=0)


@functools.lru_cache(maxsize=None)
def transform_tables(length, height):
    j = np.arange(height)
    angles = (j[:, None] * j[None, :] % height) * (2.0 * np.pi / height)
    cosine, sine = np.cos(angles), np.sin(angles)
    forward = np.concatenate(
        [np.concatenate([cosine, -sine], axis=1), np.concatenate([sine, cosine], axis=1)], axis=0
    )
    return np.stack([forward, forward.T / length]).astype(np.float32)


@functools.lru_cache(maxsize=None)
def twiddle_table(length, height):
    parts = length // height
    r = np.arange(parts)[:, None]
    j = np.arange(height)[None, :]
    angles = (j * (4 * r + 1) % (4 * length)) * (2.0 * np.pi / (4 * length))
    return np.concatenate([np.cos(angles), -np.sin(angles)], axis=1).astype(np.float32)


def turn(value, cosine, sine):
    real, imag = value
    return (real * cosine - imag * sine, real * sine + imag * cosine)


def small_fft(values, sign):
    count = len(values)
    if count == 1:
        return values
    even = small_fft(values[0::2], sign)
    odd = small_fft(values[1::2], sign)
    first, second = [], []
    for k in range(count // 2):
        real, imag = odd[k]
        if k == 0:
            pass
        elif 4 * k == count:
            real, imag = (-imag, real) if sign > 0 else (imag, -real)
        elif 8 * k == count:
            half = math.sqrt(0.5)
            if sign > 0:
                real, imag = (real - imag) * half, (real + imag) * half
            else:
                real, imag = (real + imag) * half, (imag - real) * half
        elif 8 * k == 3 * count:
            half = math.sqrt(0.5)
            if sign > 0:
                real, imag = (real + imag) * -half, (real - imag) * half
            else:
                real, imag = (imag - real) * half, (real + imag) * -half
        else:
            angle = sign * 2.0 * math.pi * k / count
            real, imag = turn((real, imag), math.cos(angle), math.sin(angle))
        base_real, base_imag = even[k]
        first.append((base_real + real, base_imag + imag))
        second.append((base_real - real, base_imag - imag))
    return first + second


def parts_forward(values):
    count = len(values)
    turned = []
    for p, value in enumerate(values):
        angle = 2.0 * math.pi * p / (4 * count)
        turned.append((value * math.cos(angle), value * -math.sin(angle)))
    return small_fft(turned, -1)


def parts_inverse(values):
    count = len(values)
    result = []
    for p, (real, imag) in enumerate(small_fft(values, 1)):
        angle = 2.0 * math.pi * p / (4 * count)
        result.append(real * math.cos(angle) - imag * math.sin(angle))
    return result


def split_bf16(value):
    high = value.astype(jnp.bfloat16)
    return high, (value - high.astype(jnp.float32)).astype(jnp.bfloat16)


def split_table(table_ref, split):
    size = table_ref.shape[1]
    for direction in range(2):
        high, low = split_bf16(table_ref[direction])
        split[direction, :size] = high
        split[direction, size : 2 * size] = high
        split[direction, 2 * size :] = low


def transform(value, split, direction):
    high, low = split_bf16(value)
    return jnp.dot(
        jnp.concatenate([high, low, high], axis=1),
        split[direction],
        preferred_element_type=jnp.float32,
    )


def spectrum_product(left, right, conjugate):
    height = left.shape[1] // 2
    left_real, left_imag = left[:, :height], left[:, height:]
    right_real, right_imag = right[:, :height], right[:, height:]
    if conjugate:
        real = left_real * right_real + left_imag * right_imag
        imag = left_real * right_imag - left_imag * right_real
    else:
        real = left_real * right_real - left_imag * right_imag
        imag = left_real * right_imag + left_imag * right_real
    return jnp.concatenate([real, imag], axis=1)


def first_chunk(load, work, twiddle_ref, index):
    parts, height = work.shape[0], work.shape[2] // 2
    row = pl.multiple_of(index * 16, 16)
    values = [load(p, row) for p in range(parts)]
    for half in (0, 8):
        rows = pl.ds(row + half, 8)
        turned = parts_forward([value[half : half + 8] for value in values])
        for r, value in enumerate(turned):
            cosine = twiddle_ref[r : r + 1, :height]
            sine = twiddle_ref[r : r + 1, height:]
            work[r, rows, :height], work[r, rows, height:] = turn(value, cosine, sine)


def last_chunk(store, work, twiddle_ref, index):
    parts, height = work.shape[0], work.shape[2] // 2
    row = pl.multiple_of(index * 16, 16)
    halves = []
    for half in (0, 8):
        rows = pl.ds(row + half, 8)
        values = []
        for r in range(parts):
            cosine = twiddle_ref[r : r + 1, :height]
            sine = twiddle_ref[r : r + 1, height:]
            value = (work[r, rows, :height], work[r, rows, height:])
            values.append(turn(value, cosine, -sine))
        halves.append(parts_inverse(values))
    for p in range(parts):
        store(p, row, jnp.concatenate([halves[0][p], halves[1][p]], axis=0))


def run_chunks(width, chunk, parts=0, block=None):
    chunks = width // 16
    group = parts // chunks if parts % chunks == 0 and parts <= 4 * chunks else 0

    def one(index, carry):
        for b in range(group):
            block(index * group + b)
        chunk(index)
        return carry

    lax.fori_loop(0, chunks, one, 0)
    if group == 0 and parts > 0:
        run_blocks(parts, block)


def run_blocks(parts, block):
    def one(index, carry):
        block(index)
        return carry

    lax.fori_loop(0, parts, one, 0)


def envelope_at(decay, start, length, height):
    position = (start + lax.broadcasted_iota(jnp.int32, (1, height), 1)).astype(jnp.float32)
    fraction = position * (1.0 / length)
    return jnp.exp(-decay * fraction), fraction


def columns_of(p, height):
    return slice(p * height, (p + 1) * height)


def filter_kernel(
    w_t_ref, hidden_ref, decay_ref, table_ref, twiddle_ref, filter_ref, spectrum_ref, work, split
):
    parts, width, height = work.shape[0], work.shape[1], work.shape[2] // 2
    length = filter_ref.shape[1]
    scale = length**-0.5
    split_table(table_ref, split)
    filter_ref[...] = jnp.dot(
        w_t_ref[...], hidden_ref[...], precision=HIGH, preferred_element_type=jnp.float32
    )

    def load(p, row):
        rows, columns = pl.ds(row, 16), columns_of(p, height)
        envelope, _ = envelope_at(decay_ref[rows, :], p * height, length, height)
        value = filter_ref[rows, columns] * envelope * scale
        filter_ref[rows, columns] = value
        return value

    def block(r):
        spectrum_ref[r] = transform(work[r], split, 0)

    run_chunks(width, lambda i: first_chunk(load, work, twiddle_ref, i))
    run_blocks(parts, block)


def main_kernel(
    both_ref,
    h_any,
    table_ref,
    twiddle_ref,
    skip_ref,
    back_ref,
    cross_any,
    work_in,
    work_grad,
    cross,
    h,
    split,
    sems,
):
    parts, width = work_in.shape[0], work_in.shape[1]
    copy_in = pltpu.make_async_copy(h_any, h, sems.at[0])
    copy_in.start()
    split_table(table_ref, split)

    def load_from(which):
        def load(p, row):
            return both_ref[p, which, pl.ds(row, 16), :].astype(jnp.float32)

        return load

    def store_to(which):
        load = load_from(which)

        def store(p, row, value):
            value = value + skip_ref[pl.ds(row, 16), :] * load(p, row)
            back_ref[p, which, pl.ds(row, 16), :] = value.astype(jnp.bfloat16)

        return store

    def block_in(r):
        spectrum = transform(work_in[r], split, 0)
        cross[r] = spectrum
        work_in[r] = transform(spectrum_product(h[r], spectrum, False), split, 1)

    def block_grad(r):
        spectrum = transform(work_grad[r], split, 0)
        cross[r] = spectrum_product(cross[r], spectrum, True)
        work_grad[r] = transform(spectrum_product(h[r], spectrum, True), split, 1)

    run_chunks(width, lambda i: first_chunk(load_from(0), work_in, twiddle_ref, i))
    copy_in.wait()
    run_chunks(
        width, lambda i: first_chunk(load_from(1), work_grad, twiddle_ref, i), parts, block_in
    )
    run_chunks(
        width, lambda i: last_chunk(store_to(0), work_in, twiddle_ref, i), parts, block_grad
    )
    copy_out = pltpu.make_async_copy(cross, cross_any, sems.at[1])
    copy_out.start()
    run_chunks(width, lambda i: last_chunk(store_to(1), work_grad, twiddle_ref, i))
    copy_out.wait()


def filter_grad_kernel(
    both_ref,
    cross_ref,
    table_ref,
    twiddle_ref,
    decay_ref,
    filter_ref,
    hidden_ref,
    w_ref,
    cosine_ref,
    positional_ref,
    small_ref,
    first_ref,
    work,
    raw,
    sums,
    split,
):
    parts, height = work.shape[0], work.shape[2] // 2
    width, length = raw.shape
    hidden_count = hidden_ref.shape[0]
    band_total = positional_ref.shape[0]
    scale = length**-0.5
    split_table(table_ref, split)

    def block(r):
        work[r] = transform(cross_ref[r], split, 1)

    def store(p, row, value):
        rows, columns = pl.ds(row, 16), columns_of(p, height)
        envelope, fraction = envelope_at(decay_ref[rows, :], p * height, length, height)
        decay_part = value * filter_ref[rows, columns] * fraction
        left = both_ref[p, 0, rows, :].astype(jnp.float32)
        right = both_ref[p, 1, rows, :].astype(jnp.float32)
        skip_part = left * right
        raw[rows, columns] = value * envelope * scale
        if p > 0:
            decay_part = decay_part + sums[0, rows, :]
            skip_part = skip_part + sums[1, rows, :]
        sums[0, rows, :] = decay_part
        sums[1, rows, :] = skip_part

    run_blocks(parts, block)
    run_chunks(width, lambda i: last_chunk(store, work, twiddle_ref, i))

    def contract_last(left, right):
        return lax.dot_general(
            left,
            right,
            (((1,), (1,)), ((), ())),
            precision=HIGH,
            preferred_element_type=jnp.float32,
        )

    second = jnp.zeros((hidden_count, width), jnp.float32)
    first = jnp.zeros((band_total, hidden_count), jnp.float32)
    chunk = min(length, 512)
    for at in range(0, length, chunk):
        columns = slice(at, at + chunk)
        grad_raw = raw[:, columns]
        second += contract_last(hidden_ref[:, columns], grad_raw)
        hidden_part = jnp.dot(
            w_ref[...], grad_raw, precision=HIGH, preferred_element_type=jnp.float32
        )
        first += contract_last(positional_ref[:, columns], hidden_part * cosine_ref[:, columns])

    first_ref[:band_total, :], first_ref[band_total:, :] = split_bf16(first * scale)
    small_ref[:hidden_count, :] = (second * scale).astype(jnp.bfloat16)
    place = lax.broadcasted_iota(jnp.int32, (16, width), 0)
    tail = jnp.zeros((16, width), jnp.float32)
    decay_pair = split_bf16(jnp.sum(sums[0].T, axis=0, keepdims=True) * -scale)
    skip_pair = split_bf16(jnp.sum(sums[1].T, axis=0, keepdims=True) * scale)
    for at, row in enumerate(decay_pair + skip_pair):
        tail = jnp.where(place == at, row.astype(jnp.float32), tail)
    small_ref[hidden_count:, :] = tail.astype(jnp.bfloat16)


def params():
    return pltpu.CompilerParams(vmem_limit_bytes=56 * MIB)


def estimate(flops, nbytes):
    return pl.CostEstimate(flops=flops, bytes_accessed=nbytes, transcendentals=0)


def gate_kernel(*refs):
    out_ref = refs[-1]
    width = out_ref.shape[2]
    for at in range(out_ref.shape[0]):
        lanes = slice(at * width, (at + 1) * width)
        for which in range(2):
            left = refs[2 * which][:, lanes].astype(jnp.float32)
            right = refs[2 * which + 1][:, lanes].astype(jnp.float32)
            out_ref[at, which] = (left * right).T.astype(jnp.bfloat16)


def gate(factors, count):
    rows, columns = factors[0].shape
    width = columns // count
    if width % 128 != 0:
        pairs = []
        for left, right in (factors[:2], factors[2:]):
            product = (left.astype(jnp.float32) * right.astype(jnp.float32)).astype(jnp.bfloat16)
            pairs.append(product.reshape(rows, count, width).transpose(1, 2, 0))
        return jnp.stack(pairs, axis=1)
    group = math.gcd(count, 4)
    return pl.pallas_call(
        gate_kernel,
        grid=(count // group,),
        in_specs=[pl.BlockSpec((rows, group * width), lambda i: (0, i))] * 4,
        out_specs=pl.BlockSpec((group, 2, width, rows), lambda i: (i, 0, 0, 0)),
        out_shape=jax.ShapeDtypeStruct((count, 2, width, rows), jnp.bfloat16),
        compiler_params=params(),
        cost_estimate=estimate(2 * rows * columns, rows * columns * 12),
    )(*factors)


def ungate_kernel(back_ref, g_ref, v_ref, k_ref, q_out, k_out, v_out):
    width = back_ref.shape[2]
    for at in range(back_ref.shape[0]):
        lanes = slice(at * width, (at + 1) * width)
        conv = back_ref[at, 0].astype(jnp.float32).T
        grad = back_ref[at, 1].astype(jnp.float32).T
        for back, factor_ref, out_ref in (
            (conv, g_ref, q_out),
            (grad, v_ref, k_out),
            (grad, k_ref, v_out),
        ):
            factor = factor_ref[:, lanes].astype(jnp.float32)
            out_ref[:, lanes] = (back * factor).astype(jnp.bfloat16)


def ungate(back, factors):
    count, _, width, rows = back.shape
    columns = count * width
    if width % 128 != 0:
        outs = []
        for which, factor in zip((0, 1, 1), factors):
            part = back[:, which].transpose(2, 0, 1).reshape(rows, columns).astype(jnp.float32)
            outs.append((part * factor.astype(jnp.float32)).astype(jnp.bfloat16))
        return outs
    group = math.gcd(count, 4)
    wide = pl.BlockSpec((rows, group * width), lambda i: (0, i))
    return pl.pallas_call(
        ungate_kernel,
        grid=(count // group,),
        in_specs=[pl.BlockSpec((group, 2, width, rows), lambda i: (i, 0, 0, 0))] + [wide] * 3,
        out_specs=[wide] * 3,
        out_shape=[jax.ShapeDtypeStruct((rows, columns), jnp.bfloat16)] * 3,
        compiler_params=params(),
        cost_estimate=estimate(3 * rows * columns, rows * columns * 16),
    )(back, *factors)


def per_device(q_proj, k_proj, v_proj, grad_out, w_first, w_second, decay_rate, skip_gain):
    height, chan_tp = q_proj.shape
    parts = lax.axis_size("seq")
    length = height * parts
    width = chan_tp // parts
    band_total, hidden_count = w_first.shape
    seq_index = lax.axis_index("seq")

    def exchange(values):
        return lax.all_to_all(values, "seq", split_axis=0, concat_axis=0, tiled=True)

    both = exchange(gate((k_proj, v_proj, grad_out, q_proj), parts))

    tables = jnp.asarray(transform_tables(length, height))
    twiddle = jnp.asarray(twiddle_table(length, height))
    positional = positional_table(length, band_total // 2)
    sine_input = jnp.dot(
        w_first.T, positional, precision=HIGH, preferred_element_type=jnp.float32
    )
    hidden = jnp.sin(sine_input)
    cosine = jnp.cos(sine_input)
    offset = seq_index * width
    w_mine = lax.dynamic_slice_in_dim(w_second, offset, width, 1)
    decay_mine = lax.dynamic_slice_in_dim(decay_rate, offset, width, 0)[:, None]
    skip_mine = lax.dynamic_slice_in_dim(skip_gain, offset, width, 0)[:, None]

    spectrum_shape = jax.ShapeDtypeStruct((parts, width, 2 * height), jnp.float32)
    work = pltpu.VMEM(spectrum_shape.shape, jnp.float32)
    split = pltpu.VMEM((2, 6 * height, 2 * height), jnp.bfloat16)
    anywhere = pl.BlockSpec(memory_space=pl.ANY)
    in_vmem = pl.BlockSpec(memory_space=pltpu.VMEM)
    product_flops = 2 * 3 * parts * 4 * height * height * width

    long_filter, filter_spectrum = pl.pallas_call(
        filter_kernel,
        in_specs=[in_vmem] * 5,
        out_specs=[in_vmem, in_vmem],
        out_shape=[jax.ShapeDtypeStruct((width, length), jnp.float32), spectrum_shape],
        scratch_shapes=[work, split],
        compiler_params=params(),
        cost_estimate=estimate(product_flops, length * width * 12),
    )(w_mine.T, hidden, decay_mine, tables, twiddle)

    back, cross = pl.pallas_call(
        main_kernel,
        in_specs=[in_vmem, anywhere, in_vmem, in_vmem, in_vmem],
        out_specs=[in_vmem, anywhere],
        out_shape=[jax.ShapeDtypeStruct(both.shape, jnp.bfloat16), spectrum_shape],
        scratch_shapes=[work, work, work, work, split, pltpu.SemaphoreType.DMA((2,))],
        compiler_params=params(),
        cost_estimate=estimate(4 * product_flops, length * width * 32),
    )(both, filter_spectrum, tables, twiddle, skip_mine)
    back = exchange(back)

    small, first_pair = pl.pallas_call(
        filter_grad_kernel,
        in_specs=[in_vmem] * 10,
        out_specs=[in_vmem, in_vmem],
        out_shape=[
            jax.ShapeDtypeStruct((hidden_count + 16, width), jnp.bfloat16),
            jax.ShapeDtypeStruct((2 * band_total, hidden_count), jnp.bfloat16),
        ],
        scratch_shapes=[
            work,
            pltpu.VMEM((width, length), jnp.float32),
            pltpu.VMEM((2, width, height), jnp.float32),
            split,
        ],
        compiler_params=params(),
        cost_estimate=estimate(2 * product_flops, length * width * 30),
    )(
        both,
        cross,
        tables,
        twiddle,
        decay_mine,
        long_filter,
        hidden,
        w_mine,
        cosine,
        positional,
    )
    packed = jnp.concatenate([small, first_pair.reshape(-1, width)], axis=0)
    gathered = lax.all_gather(packed, "seq", axis=1, tiled=True)
    grad_second = gathered[:hidden_count].astype(jnp.float32)
    tail = gathered[hidden_count : hidden_count + 4].astype(jnp.float32)
    grad_decay = tail[0] + tail[1]
    grad_skip = tail[2] + tail[3]
    first_rows = gathered[hidden_count + 16 :].astype(jnp.float32)
    first_rows = first_rows.reshape(-1, parts, width).sum(axis=1)
    grad_first = first_rows.reshape(2, band_total, hidden_count).sum(axis=0)
    if lax.axis_size("tp") == 2:
        grad_first = grad_first + lax.ppermute(grad_first, "tp", [(0, 1), (1, 0)])
    else:
        grad_first = lax.psum(grad_first, "tp")
    grad_q, grad_k, grad_v = ungate(back, (grad_out, v_proj, k_proj))
    return (grad_q, grad_k, grad_v, grad_first, grad_second, grad_decay, grad_skip)


def solution(mesh):
    return jax.shard_map(
        per_device,
        mesh=mesh,
        in_specs=(
            P("seq", "tp"),
            P("seq", "tp"),
            P("seq", "tp"),
            P("seq", "tp"),
            P(),
            P(None, "tp"),
            P("tp"),
            P("tp"),
        ),
        out_specs=(
            P("seq", "tp"),
            P("seq", "tp"),
            P("seq", "tp"),
            P(),
            P(None, "tp"),
            P("tp"),
            P("tp"),
        ),
        check_vma=False,
    )
```

time: 172 us -> 184 us (1.070)
  local copies, waits for them, and re-layouts: 40.3 us -> 9.04 us
  blocking collectives: 34.7 us -> 58.4 us
  Pallas kernels: 47.7 us -> 65.5 us
    unnamed x58 -> x13, local copies, waits for them, and re-layouts: 31.8 us -> 3.62 us
    all_gather x1, blocking collectives: 34.7 us -> 58.4 us  [per_device(): gathered = lax.all_gather(packed, 'seq', axis=1, tiled=True)]
    pallas_call x1, Pallas kernels: 22.6 us -> 27.9 us  [per_device(): pl.pallas_call(main_kernel, in_specs=[in_vmem, anywhere, in_vmem, in_vmem...]
    pallas_call x1, Pallas kernels: 8.73 us -> 13 us  [per_device(): pl.pallas_call(filter_kernel, in_specs=[in_vmem] * 5, out_specs=[in_vmem,...]
    pallas_call x1, Pallas kernels: 0.87 us -> 4.61 us  [gate(): pl.pallas_call(gate_kernel, grid=(count // group,), in_specs=[pl.BlockSpe...]
    pallas_call x1, Pallas kernels: 11.4 us -> 15 us  [per_device(): pl.pallas_call(filter_grad_kernel, in_specs=[in_vmem] * 10, out_specs=[in...]
    cos x1 -> x0, local copies, waits for them, and re-layouts: 2.36 us -> none  [per_device(): cosine = jnp.cos(sine_input)]
    sin x1 -> x0, local copies, waits for them, and re-layouts: 2.35 us -> none  [per_device(): hidden = jnp.sin(sine_input)]
  transfers between devices with their start and end apart: 3 -> 3, of which waited for: 1 -> 1; matrix products, arithmetic and copies ran while one was open for 10% -> 8% of each run, Pallas kernels for 12% -> 7%
where the time goes in v1:
time: 184 us; the launch traced here: 182 us
  Pallas kernels  65.5 us (36%)
  blocking collectives  58.4 us (32%)
  starting transfers between devices  20.4 us (11%)
  waiting for transfers between devices  18.7 us (10%)
  local copies, waits for them, and re-layouts  9.04 us (5%)
  other arithmetic  5.58 us (3%)
  matrix products  3.45 us (2%)
    all_gather x1, blocking collectives, per_device(): gathered = lax.all_gather(packed, 'seq', axis=1, tiled=True)  58.4 us
    pallas_call x1, Pallas kernels, per_device(): pl.pallas_call(main_kernel, in_specs=[in_vmem, anywhere, in_vmem, in_vmem...  27.9 us
    all_to_all x2, starting transfers between devices, exchange(): lax.all_to_all(values, 'seq', split_axis=0, concat_axis=0, tiled=True)  18.9 us
    all_to_all x2, waiting for transfers between devices, exchange(): lax.all_to_all(values, 'seq', split_axis=0, concat_axis=0, tiled=True)  18.7 us
    pallas_call x1, Pallas kernels, per_device(): pl.pallas_call(filter_grad_kernel, in_specs=[in_vmem] * 10, out_specs=[in...  15 us
    pallas_call x1, Pallas kernels, per_device(): pl.pallas_call(filter_kernel, in_specs=[in_vmem] * 5, out_specs=[in_vmem,...  13 us
    pallas_call x1, Pallas kernels, ungate(): pl.pallas_call(ungate_kernel, grid=(count // group,), in_specs=[pl.BlockS...  4.94 us
    pallas_call x1, Pallas kernels, gate(): pl.pallas_call(gate_kernel, grid=(count // group,), in_specs=[pl.BlockSpe...  4.61 us
  transfers between devices with their start and end apart: 3, of which 1 were waited for; matrix products, arithmetic and copies ran while one was open for 8% of the time, Pallas kernels for 7%

profile of v1, /device:TPU:0, one launch (start us, length us, event | category | flops | bytes accessed | tf_op | source)
XLA Modules:
  0.0 181.8 jit_solution(16861437184270206984)
XLA Ops:
  0.6 0.0 copy-start
  0.6 4.6 %shard_map.153 = bf16[16,2,256,128]{3,2,1,0:T(8,128)(2,1)} custom-call(bf16[128,4096]{1,0:T(8,128)(2,1)} %k_ref.1, bf16[128,4096]{1,0:T(8,128)(2,1)} %v_ref.1, bf16[128,4096]{1,0:T(8,128)(2,1)} %g_ref.1, bf16[128,4096]{1,0:T(8,128)(2,1)} %refs_3_.1), custom_call_target="tpu_custom_call" | custom-call | flops 1048576 | bytes 6291456 | tf_op jit(solution)/shard_map/pallas_call | solution.py:392
  5.3 7.5 %all-to-all-start = ((bf16[16,2,256,128]{3,2,1,0:T(8,128)(2,1)}), bf16[16,2,256,128]{3,2,1,0:T(8,128)(2,1)S(1)}, u32[]{:S(2)}, u32[]{:S(2)}) async-start(bf16[16,2,256,128]{3,2,1,0:T(8,128)(2,1)} %shard_map.153), calls=%async_computation | async-start | bytes 4194304 | tf_op jit(solution)/shard_map/all_to_all | solution.py:449
  12.8 0.8 dynamic_slice.10
  13.6 0.8 copy.23.decay_ref
  14.4 0.8 copy.22.w_t_ref
  15.1 0.8 dynamic_slice.11
  15.9 0.8 copy.24.skip_ref
  16.7 0.6 constant_dynamic-slice_fusion.w_ref
  17.3 0.6 fusion.7
  17.9 3.4 %cosine_bitcast_fusion = (f32[64,2048]{1,0:T(8,128)}, f32[64,2048]{1,0:T(8,128)}) fusion(f32[32,64]{1,0:T(8,128)S(1)} %copy-done.5, f32[16,2048]{1,0:T(8,128)S(1)} %get-tuple-element.30, f32[16,2048]{1,0:T(8,128)S(1)} %get-tuple-element.29), kind=kOutput, calls=%fused_computation.1 | convolution fusion | flops 50397184 | bytes 1318912 | tf_op jit(solution)/shard_map/dot_general | solution.py:456
  21.4 13.0 %shard_map.154 = (f32[256,2048]{1,0:T(8,128)}, f32[16,256,256]{2,1,0:T(8,128)}) custom-call(f32[256,64]{1,0:T(8,128)} %copy.22.w_t_ref, f32[64,2048]{1,0:T(8,128)} %get-tuple-element.26.hidden_ref, f32[256,1]{1,0:T(8,128)} %copy.23.decay_ref, f32[2,256,256]{2,1,0:T(8,128)} %constant.38.clone.table_ref, f32[16,256]{1,0:T(8,128)} %constant.39.clone.twiddle_ref), custom_call_target="tpu_custom_call" | custom-call | flops 1610612736 | bytes 6291456 | tf_op jit(solution)/shard_map/pallas_call | solution.py:473
  34.4 0.7 pad_maximum_fusion.positional_ref
  35.2 18.7 %all-to-all-done.both_ref = bf16[16,2,256,128]{3,2,1,0:T(8,128)(2,1)S(1)} async-done(((bf16[16,2,256,128]{3,2,1,0:T(8,128)(2,1)}), bf16[16,2,256,128]{3,2,1,0:T(8,128)(2,1)S(1)}, u32[]{:S(2)}, u32[]{:S(2)}) %all-to-all-start) | async-done | bytes 2097184 | tf_op jit(solution)/shard_map/all_to_all | solution.py:449
  53.9 1.3 copy-done.3
  55.2 27.9 %shard_map.155 = (bf16[16,2,256,128]{3,2,1,0:T(8,128)(2,1)}, f32[16,256,256]{2,1,0:T(8,128)}) custom-call(bf16[16,2,256,128]{3,2,1,0:T(8,128)(2,1)} %copy-done.3, f32[16,256,256]{2,1,0:T(8,128)} %get-tuple-element.16.h_any, f32[2,256,256]{2,1,0:T(8,128)} %constant.38.clone.table_ref, f32[16,256]{1,0:T(8,128)} %constant.39.clone.twiddle_ref, ...), custom_call_target="tpu_custom_call" | custom-call | flops 6442450944 | bytes 16777216 | tf_op jit(solution)/shard_map/pallas_call | solution.py:483
  83.1 15.0 %shard_map.157 = (bf16[80,256]{1,0:T(8,128)(2,1)}, bf16[64,64]{1,0:T(8,128)(2,1)}) custom-call(bf16[16,2,256,128]{3,2,1,0:T(8,128)(2,1)} %copy-done.3, f32[16,256,256]{2,1,0:T(8,128)} %get-tuple-element.21.cross_ref, f32[2,256,256]{2,1,0:T(8,128)} %constant.38.clone.table_ref, f32[16,256]{1,0:T(8,128)} %constant.39.clone.twiddle_ref, ...), custom_call_target="tpu_custom_call" | custom-call | flops 3221225472 | bytes 15728640 | tf_op jit(solution)/shard_map/pallas_call | solution.py:494
  98.1 0.8 reshape.36
  98.9 11.4 %all-to-all-start.1 = ((bf16[16,2,256,128]{3,2,1,0:T(8,128)(2,1)}), bf16[16,2,256,128]{3,2,1,0:T(8,128)(2,1)S(1)}, u32[]{:S(2)}, u32[]{:S(2)}) async-start(bf16[16,2,256,128]{3,2,1,0:T(8,128)(2,1)} %get-tuple-element.17), calls=%async_computation.1 | async-start | bytes 4194304 | tf_op jit(solution)/shard_map/all_to_all | solution.py:449
  110.3 58.4 %all_gather.3 = bf16[96,4096]{1,0:T(8,128)(2,1)S(1)} all-gather(bf16[96,256]{1,0:T(8,128)(2,1)S(1)} %pad_maximum_fusion.1), channel_id=1, replica_groups=mesh['seq'=16,'tp'=2] {'seq'}, dimensions={1}, use_global_device_ids=true | all-gather | bytes 835584 | tf_op jit(solution)/shard_map/all_gather | solution.py:523
  168.7 0.9 copy-done.2
  169.6 0.1 copy.26
  169.7 0.1 reshape.39
  169.8 1.6 collective-permute-start
  171.3 0.8 slice_convert_fusion.2
  172.2 2.1 %slice_convert_fusion = f32[64,4096]{1,0:T(8,128)} fusion(bf16[96,4096]{1,0:T(8,128)(2,1)} %copy-done.2), kind=kLoop, calls=%fused_computation | loop fusion | flops 262144 | bytes 1572864 | tf_op jit(solution)/shard_map/convert_element_type | solution.py:524
  174.3 0.6 slice_add_fusion
  174.9 0.0 collective-permute-done
  174.9 0.6 add.51
  175.5 0.0 all-to-all-done.1.back_ref
  175.5 1.3 copy-done.1
  176.9 4.9 %shard_map.156 = (bf16[128,4096]{1,0:T(8,128)(2,1)}, bf16[128,4096]{1,0:T(8,128)(2,1)}, bf16[128,4096]{1,0:T(8,128)(2,1)}) custom-call(bf16[16,2,256,128]{3,2,1,0:T(8,128)(2,1)} %copy-done.1, bf16[128,4096]{1,0:T(8,128)(2,1)} %g_ref.1, bf16[128,4096]{1,0:T(8,128)(2,1)} %v_ref.1, bf16[128,4096]{1,0:T(8,128)(2,1)} %k_ref.1), custom_call_target="tpu_custom_call" | custom-call | flops 1572864 | bytes 8388608 | tf_op jit(solution)/shard_map/pallas_call | solution.py:429
  (14 shorter events, 0.1 us)
Async XLA Ops:
  0.6 13.7 %copy-start = (f32[64,4096]{1,0:T(8,128)S(1)}, f32[64,4096]{1,0:T(8,128)}, u32[]{:S(2)}) copy-start(f32[64,4096]{1,0:T(8,128)} %param.15) | copy-start | bytes 3145732
  5.3 12.7 %copy-start.5 = (f32[32,64]{1,0:T(8,128)S(1)}, f32[32,64]{1,0:T(8,128)}, u32[]{:S(2)}) copy-start(f32[32,64]{1,0:T(8,128)} %param.14) | copy-start | bytes 24580
  5.3 48.6 %all-to-all-start = ((bf16[16,2,256,128]{3,2,1,0:T(8,128)(2,1)}), bf16[16,2,256,128]{3,2,1,0:T(8,128)(2,1)S(1)}, u32[]{:S(2)}, u32[]{:S(2)}) async-start(bf16[16,2,256,128]{3,2,1,0:T(8,128)(2,1)} %shard_map.153), calls=%async_computation | async-start | bytes 4194304 | tf_op jit(solution)/shard_map/all_to_all | solution.py:449
  53.9 1.3 copy-start.3
  98.9 11.4 %copy-start.4 = (bf16[80,256]{1,0:T(8,128)(2,1)S(1)}, bf16[80,256]{1,0:T(8,128)(2,1)}, u32[]{:S(2)}) copy-start(bf16[80,256]{1,0:T(8,128)(2,1)} %get-tuple-element.23) | copy-start | bytes 122884
  98.9 76.6 %all-to-all-start.1 = ((bf16[16,2,256,128]{3,2,1,0:T(8,128)(2,1)}), bf16[16,2,256,128]{3,2,1,0:T(8,128)(2,1)S(1)}, u32[]{:S(2)}, u32[]{:S(2)}) async-start(bf16[16,2,256,128]{3,2,1,0:T(8,128)(2,1)} %get-tuple-element.17), calls=%async_computation.1 | async-start | bytes 4194304 | tf_op jit(solution)/shard_map/all_to_all | solution.py:449
  168.7 0.9 copy-start.2
  169.8 5.1 %collective-permute-start = (f32[32,64]{1,0:T(8,128)S(1)}, f32[32,64]{1,0:T(8,128)S(1)}, u32[]{:S(2)}, u32[]{:S(2)}) collective-permute-start(f32[32,64]{1,0:T(8,128)S(1)} %reduce_sum.19), channel_id=1, source_target_pairs={{0,1},{1,0},{2,3},{3,2},{4,5},{5,4},{6,7},{7,6},{8,9},{9,8},{10,11... | collective-permute-start | bytes 24584 | tf_op jit(solution)/shard_map/ppermute | solution.py:532
  175.5 1.3 copy-start.1
